TPU v7x, 128 devices: a whole 4x4x4 slice. The times are simulated.
128 devices in a mesh: ctx: 32 (over x, y, core), head: 4 (over z).
Axes of the slice: x: 4, y: 4, z: 4, core: 2. Of those that a mesh axis runs over, the one named last changes fastest.
Arguments:
- query: bfloat16 [4, 8192], P(None, 'head'), may hold values from -8 to 8
- key_cache: bfloat16 [4, 131072, 1024], P(None, 'ctx', 'head'), may hold values from -80 to 80
- cached_value_matrix: bfloat16 [4, 131072, 1024], P(None, 'ctx', 'head'), may hold values from -24 to 24
- lengths: int32 [4], replicated, may hold values from 2 to 131072, as said below
- out_weight: bfloat16 [8192, 8192], P('head', 'ctx'), may hold values from -0.0625 to 0.0625
Outputs:
- projected: float32 [4, 8192], P(None, 'ctx')
Inputs may be any that keep to these rules, and one draw needn't show every extreme that they name: `lengths`: some sequence has exactly 131072 valid positions in every draw.
All inputs are finite; a program needn't handle non-finite values.
Results may differ from a plain program's by a relative error of at most 0.0095.
Values sent between devices are 32-bit elements; how exact they have to be, the bound alone decides.
No kernel may reach another device: no remote copies, remote signals or barrier semaphores. Data moves between devices by JAX's collectives and lax.ppermute only.
A program may use at most 64 MiB of HBM per device.

v0:
```python
import functools

import jax
import jax.numpy as jnp
from jax import lax
from jax.experimental import pallas as pl
from jax.experimental.pallas import tpu as pltpu
from jax.sharding import PartitionSpec as P

HEAD_WIDTH = 128
LOWEST = -1e30
LOG2_E = 1.4426950408889634
PACKED = 72
MIB = 1 << 20


def attention_kernel(lengths_hbm, query_hbm, key_hbm, value_hbm, out_ref,
                     lengths, order, query, query_rows, blocks, keys, values, scores, weights, tops, totals, mixes,
                     small_sem, key_sem, value_sem):
    rows, ctx_dev, _ = keys.shape
    heads = query_rows.shape[1]
    group = heads // 2
    span = ctx_dev // 2

    def key_copy(r, c):
        piece = pl.ds(c * span, span)
        return pltpu.make_async_copy(key_hbm.at[r, piece], keys.at[r, piece], key_sem.at[r, c])

    def value_copy(r, c):
        piece = pl.ds(c * span, span)
        return pltpu.make_async_copy(value_hbm.at[r, piece], values.at[r, piece], value_sem.at[r, c])

    lengths_copy = pltpu.make_async_copy(lengths_hbm, lengths, small_sem.at[1])
    query_copy = pltpu.make_async_copy(query_hbm, query, small_sem.at[0])
    lengths_copy.start()
    query_copy.start()
    for c in range(2):
        key_copy(0, c).start()

    offset = lax.axis_index("ctx") * ctx_dev
    lengths_copy.wait()
    count = jnp.int32(0)
    for r in range(rows):
        order[count] = r
        count += (lengths[r] > offset).astype(jnp.int32)
    first_ready = lengths[0] > offset

    def start_keys(i, c):
        @pl.when(i < count)
        def _():
            key_copy(order[i], c).start()

    def start_values(i, c):
        @pl.when(i < count)
        def _():
            value_copy(order[i], c).start()

    @pl.when(jnp.logical_not(first_ready))
    def _():
        start_keys(0, 0)
        start_keys(0, 1)

    for c in range(2):
        start_keys(1, c)
        start_values(0, c)

    query_copy.wait()
    wide = query[...].astype(jnp.float32)
    for h in range(heads):
        query_rows[:, h, :] = wide[:, h * HEAD_WIDTH:(h + 1) * HEAD_WIDTH]
    nothing = jnp.zeros((group, HEAD_WIDTH), jnp.float32)
    for r in range(rows):
        blocks[r] = jnp.concatenate(
            [
                jnp.concatenate([query_rows[r, :group], nothing], axis=1),
                jnp.concatenate([nothing, query_rows[r, group:]], axis=1),
            ],
            axis=0,
        ).astype(jnp.bfloat16)
    tops[...] = jnp.full(tops.shape, LOWEST, jnp.float32)
    totals[...] = jnp.zeros(totals.shape, jnp.float32)
    mixes[...] = jnp.zeros(mixes.shape, jnp.float32)
    place = lax.broadcasted_iota(jnp.int32, (heads, span), 1)

    def score(r, c):
        scores[c] = lax.dot_general(
            blocks[r], keys[r, c * span:(c + 1) * span], (((1,), (1,)), ((), ())),
            preferred_element_type=jnp.float32,
        )

    def weigh(r, c):
        valid = place < lengths[r] - offset - c * span
        scaled = jnp.where(valid, scores[c] * jnp.float32(LOG2_E / HEAD_WIDTH**0.5), jnp.float32(LOWEST))
        top = jnp.max(scaled, axis=1, keepdims=True)
        weight = jnp.where(valid, jnp.exp2(scaled - top), jnp.float32(0.0))
        weights[c] = weight.astype(jnp.bfloat16)
        tops[r, c] = jnp.broadcast_to(top, (heads, HEAD_WIDTH))
        totals[r, c] = jnp.broadcast_to(jnp.sum(weight, axis=1, keepdims=True), (heads, HEAD_WIDTH))

    def mix(r, c):
        both = jnp.dot(weights[c], values[r, c * span:(c + 1) * span], preferred_element_type=jnp.float32)
        mixes[r, c] = jnp.concatenate([both[:group, :HEAD_WIDTH], both[group:, HEAD_WIDTH:]], axis=0)

    def go_on(i, c):
        start_keys(i + 2, c)
        start_values(i + 1, c)

    r = order[0]
    key_copy(r, 0).wait()
    go_on(0, 0)
    score(r, 0)
    key_copy(r, 1).wait()
    go_on(0, 1)
    score(r, 1)
    weigh(r, 0)

    def step(i, last):
        r = order[i]
        key_copy(r, 0).wait()
        value_copy(last, 0).wait()
        go_on(i, 0)
        mix(last, 0)
        weigh(last, 1)
        score(r, 0)
        key_copy(r, 1).wait()
        value_copy(last, 1).wait()
        go_on(i, 1)
        mix(last, 1)
        weigh(r, 0)
        score(r, 1)
        return r

    last = lax.fori_loop(1, count, step, r)
    value_copy(last, 0).wait()
    mix(last, 0)
    weigh(last, 1)
    value_copy(last, 1).wait()
    mix(last, 1)

    @pl.when(jnp.logical_not(first_ready))
    def _():
        for c in range(2):
            key_copy(0, c).wait()

    top = jnp.maximum(tops[:, 0], tops[:, 1])
    scales = [jnp.exp2(tops[:, c] - top) for c in range(2)]
    total = totals[:, 0] * scales[0] + totals[:, 1] * scales[1]
    mixed = mixes[:, 0] * scales[0] + mixes[:, 1] * scales[1]
    half = rows * heads
    top, total, mixed = (x.reshape(half, HEAD_WIDTH) for x in (top, total, mixed))
    lane = lax.broadcasted_iota(jnp.int32, (half, HEAD_WIDTH), 1)
    stats = jnp.where(lane == 0, top, total)
    turned = jnp.concatenate([mixed, mixed], axis=0).T
    out_ref[:half] = jnp.where(lane < half, turned[:half], turned[half:])
    out_ref[half:] = jnp.concatenate([stats, stats], axis=0).T[:8]


def attention(query, key_cache, value_cache, lengths):
    rows, ctx_dev, kv_cols = key_cache.shape
    heads = query.shape[1] // HEAD_WIDTH
    span = ctx_dev // 2
    hbm = pl.BlockSpec(memory_space=pltpu.HBM)
    return pl.pallas_call(
        attention_kernel,
        out_shape=jax.ShapeDtypeStruct((PACKED, HEAD_WIDTH), jnp.float32),
        in_specs=[hbm] * 4,
        out_specs=pl.BlockSpec(memory_space=pltpu.VMEM),
        scratch_shapes=[
            pltpu.SMEM((rows,), jnp.int32),
            pltpu.SMEM((rows + 1,), jnp.int32),
            pltpu.VMEM(query.shape, jnp.bfloat16),
            pltpu.VMEM((rows, heads, HEAD_WIDTH), jnp.float32),
            pltpu.VMEM((rows, heads, 2 * HEAD_WIDTH), jnp.bfloat16),
            pltpu.VMEM(key_cache.shape, jnp.bfloat16),
            pltpu.VMEM(value_cache.shape, jnp.bfloat16),
            pltpu.VMEM((2, heads, span), jnp.float32),
            pltpu.VMEM((2, heads, span), jnp.bfloat16),
            pltpu.VMEM((rows, 2, heads, HEAD_WIDTH), jnp.float32),
            pltpu.VMEM((rows, 2, heads, HEAD_WIDTH), jnp.float32),
            pltpu.VMEM((rows, 2, heads, HEAD_WIDTH), jnp.float32),
            pltpu.SemaphoreType.DMA((2,)),
            pltpu.SemaphoreType.DMA((rows, 2)),
            pltpu.SemaphoreType.DMA((rows, 2)),
        ],
        compiler_params=pltpu.CompilerParams(vmem_limit_bytes=54 * MIB),
        cost_estimate=pl.CostEstimate(
            flops=4 * rows * heads * ctx_dev * kv_cols, bytes_accessed=4 * rows * ctx_dev * kv_cols, transcendentals=0
        ),
    )(lengths, query, key_cache, value_cache)


def fetch_kernel(source, target, sem):
    copy = pltpu.make_async_copy(source, target, sem)
    copy.start()
    copy.wait()


def fetch(packed):
    return pl.pallas_call(
        fetch_kernel,
        out_shape=jax.ShapeDtypeStruct(packed.shape, packed.dtype),
        in_specs=[pl.BlockSpec(memory_space=pltpu.HBM)],
        out_specs=pl.BlockSpec(memory_space=pltpu.VMEM),
        scratch_shapes=[pltpu.SemaphoreType.DMA],
        compiler_params=pltpu.CompilerParams(vmem_limit_bytes=4 * MIB),
        cost_estimate=pl.CostEstimate(flops=0, bytes_accessed=packed.size * 4, transcendentals=0),
    )(packed)


def merge(pieces):
    half = PACKED - 8
    tops = [p[half:half + 1] for p in pieces]
    top = functools.reduce(jnp.maximum, tops)
    scales = [jnp.exp2(t - top) for t in tops]
    mixed = sum(p[:half] * s for p, s in zip(pieces, scales))
    total = sum(p[half + 1:half + 2] * s for p, s in zip(pieces, scales))
    return mixed, top, total


def merge_kernel(*refs):
    out_ref = refs[-1]
    mixed, top, total = merge([ref[...] for ref in refs[:-1]])
    half = mixed.shape[0]
    out_ref[:half] = mixed
    row = lax.broadcasted_iota(jnp.int32, (8, HEAD_WIDTH), 0)
    out_ref[half:] = jnp.where(row == 0, top, total)


def merge_call(pieces):
    vmem = pl.BlockSpec(memory_space=pltpu.VMEM)
    return pl.pallas_call(
        merge_kernel,
        out_shape=jax.ShapeDtypeStruct((PACKED, HEAD_WIDTH), jnp.float32),
        in_specs=[vmem] * len(pieces),
        out_specs=vmem,
        compiler_params=pltpu.CompilerParams(vmem_limit_bytes=4 * MIB),
    )(*pieces)


def project_kernel(rows, heads, *refs):
    *pieces, weight_ref, out_ref, attended = refs
    mixed, _, total = merge([ref[...] for ref in pieces])
    mixed = mixed / total
    half = mixed.shape[0]
    attended[...] = jnp.concatenate([mixed, pltpu.roll(mixed, half, 1)], axis=0).T[:half]
    flat = jnp.concatenate([attended[pl.ds(h, rows, stride=heads), :] for h in range(heads)], axis=1)
    out_ref[...] = jnp.dot(flat.astype(jnp.bfloat16), weight_ref[...], preferred_element_type=jnp.float32)


def project_call(pieces, out_weight, rows):
    heads = out_weight.shape[0] // HEAD_WIDTH
    vmem = pl.BlockSpec(memory_space=pltpu.VMEM)
    return pl.pallas_call(
        functools.partial(project_kernel, rows, heads),
        out_shape=jax.ShapeDtypeStruct((rows, out_weight.shape[1]), jnp.float32),
        in_specs=[vmem] * (len(pieces) + 1),
        out_specs=vmem,
        scratch_shapes=[pltpu.VMEM((rows * heads, HEAD_WIDTH), jnp.float32)],
        compiler_params=pltpu.CompilerParams(vmem_limit_bytes=16 * MIB),
    )(*pieces, out_weight)


def exchange(value, axis, bits):
    size = lax.axis_size(axis)
    return [value] + [lax.ppermute(value, axis, [(i, i ^ bit) for i in range(size)]) for bit in bits]


def on_device(query, key_cache, cached_value_matrix, lengths, out_weight):
    rows = query.shape[0]
    packed = attention(query, key_cache, cached_value_matrix, lengths)
    packed = merge_call([fetch(packed)] + exchange(packed, "ctx", (1,))[1:])
    packed = merge_call(exchange(packed, "ctx", (3, 7, 5)))
    partial_value = project_call(exchange(packed, "ctx", (17, 25, 9)), out_weight, rows)
    return functools.reduce(jnp.add, exchange(partial_value, "head", (1, 3, 2)))


def solution(mesh):
    in_specs = (
        P(None, "head"),
        P(None, "ctx", "head"),
        P(None, "ctx", "head"),
        P(),
        P("head", "ctx"),
    )
    out_specs = P(None, "ctx")
    return jax.shard_map(
        on_device, mesh=mesh, in_specs=in_specs, out_specs=out_specs, check_vma=False
    )
```

profile of v0, /device:TPU:0, one launch (start us, length us, event | category | flops | bytes accessed | tf_op | source)
XLA Modules:
  0.0 32.9 jit_solution(2760049090724084472)
XLA Ops:
  0.0 0.0 copy-start
  0.0 7.8 %shard_map.55.source = f32[72,128]{1,0:T(8,128)} custom-call(s32[4]{0:T(128)} %lengths_hbm.1, bf16[4,2048]{1,0:T(4,128)(2,1)} %query_hbm.1, bf16[4,4096,256]{2,1,0:T(8,128)(2,1)} %key_hbm.1, bf16[4,4096,256]{2,1,0:T(8,128)(2,1)} %value_hbm.1), custom_call_target="tpu_custom_call" | custom-call | flops 268435456 | bytes 16777216 | tf_op jit(solution)/shard_map/pallas_call | solution.py:163
  7.8 0.1 collective-permute-start
  7.9 0.0 copy-start.1
  7.9 0.8 %copy-done.1 = f32[72,128]{1,0:T(8,128)S(1)} copy-done((f32[72,128]{1,0:T(8,128)S(1)}, f32[72,128]{1,0:T(8,128)}, u32[]{:S(2)}) %copy-start.1) | copy-done | bytes 36888
  8.7 0.6 %collective-permute-done.refs_1_ = f32[72,128]{1,0:T(8,128)S(1)} collective-permute-done((f32[72,128]{1,0:T(8,128)}, f32[72,128]{1,0:T(8,128)S(1)}, u32[]{:S(2)}, u32[]{:S(2)}) %collective-permute-start) | collective-permute-done | bytes 36896 | tf_op jit(solution)/shard_map/ppermute | solution.py:265
  9.3 3.1 %collective-permute-start.3 = (f32[72,128]{1,0:T(8,128)S(1)}, f32[72,128]{1,0:T(8,128)S(1)}, u32[]{:S(2)}, u32[]{:S(2)}) collective-permute-start(f32[72,128]{1,0:T(8,128)S(1)} %shard_map.57.refs_0_), channel_id=1, source_target_pairs={{0,20},{4,16},{8,28},{12,24},{16,4},{20,0},{24,12},{28,8},{32,52},... | collective-permute-start | bytes 110600 | tf_op jit(solution)/shard_map/ppermute | solution.py:265
  12.4 1.0 %collective-permute-start.2 = (f32[72,128]{1,0:T(8,128)S(1)}, f32[72,128]{1,0:T(8,128)S(1)}, u32[]{:S(2)}, u32[]{:S(2)}) collective-permute-start(f32[72,128]{1,0:T(8,128)S(1)} %shard_map.57.refs_0_), channel_id=1, source_target_pairs={{0,28},{4,24},{8,20},{12,16},{16,12},{20,8},{24,4},{28,0},{32,60},... | collective-permute-start | bytes 110600 | tf_op jit(solution)/shard_map/ppermute | solution.py:265
  13.4 0.0 collective-permute-start.1
  13.4 0.9 %collective-permute-done.3.refs_3_ = f32[72,128]{1,0:T(8,128)S(1)} collective-permute-done((f32[72,128]{1,0:T(8,128)S(1)}, f32[72,128]{1,0:T(8,128)S(1)}, u32[]{:S(2)}, u32[]{:S(2)}) %collective-permute-start.3) | collective-permute-done | bytes 36896 | tf_op jit(solution)/shard_map/ppermute | solution.py:265
  14.3 2.7 %collective-permute-done.2.refs_2_ = f32[72,128]{1,0:T(8,128)S(1)} collective-permute-done((f32[72,128]{1,0:T(8,128)S(1)}, f32[72,128]{1,0:T(8,128)S(1)}, u32[]{:S(2)}, u32[]{:S(2)}) %collective-permute-start.2) | collective-permute-done | bytes 36896 | tf_op jit(solution)/shard_map/ppermute | solution.py:265
  17.0 0.0 collective-permute-done.1.refs_1_
  17.1 1.2 %collective-permute-start.6 = (f32[72,128]{1,0:T(8,128)S(1)}, f32[72,128]{1,0:T(8,128)S(1)}, u32[]{:S(2)}, u32[]{:S(2)}) collective-permute-start(f32[72,128]{1,0:T(8,128)S(1)} %shard_map.58.refs_0_), channel_id=1, source_target_pairs={{0,36},{4,32},{8,44},{12,40},{16,52},{20,48},{24,60},{28,56},{32,4... | collective-permute-start | bytes 110600 | tf_op jit(solution)/shard_map/ppermute | solution.py:265
  18.2 0.0 collective-permute-start.5
  18.2 2.7 %collective-permute-start.4 = (f32[72,128]{1,0:T(8,128)S(1)}, f32[72,128]{1,0:T(8,128)S(1)}, u32[]{:S(2)}, u32[]{:S(2)}) collective-permute-start(f32[72,128]{1,0:T(8,128)S(1)} %shard_map.58.refs_0_), channel_id=1, source_target_pairs={{0,68},{4,64},{8,76},{12,72},{16,84},{20,80},{24,92},{28,88},{32,1... | collective-permute-start | bytes 110600 | tf_op jit(solution)/shard_map/ppermute | solution.py:265
  20.9 0.0 collective-permute-done.6.refs_3_
  20.9 1.9 %collective-permute-done.5.refs_2_ = f32[72,128]{1,0:T(8,128)S(1)} collective-permute-done((f32[72,128]{1,0:T(8,128)S(1)}, f32[72,128]{1,0:T(8,128)S(1)}, u32[]{:S(2)}, u32[]{:S(2)}) %collective-permute-start.5) | collective-permute-done | bytes 36896 | tf_op jit(solution)/shard_map/ppermute | solution.py:265
  22.8 0.4 %collective-permute-done.4.refs_1_ = f32[72,128]{1,0:T(8,128)S(1)} collective-permute-done((f32[72,128]{1,0:T(8,128)S(1)}, f32[72,128]{1,0:T(8,128)S(1)}, u32[]{:S(2)}, u32[]{:S(2)}) %collective-permute-start.4) | collective-permute-done | bytes 36896 | tf_op jit(solution)/shard_map/ppermute | solution.py:265
  23.2 0.0 copy-done
  23.2 0.4 %shard_map.59 = f32[4,256]{1,0:T(4,128)S(1)} custom-call(f32[72,128]{1,0:T(8,128)S(1)} %shard_map.58.refs_0_, f32[72,128]{1,0:T(8,128)S(1)} %collective-permute-done.4.refs_1_, f32[72,128]{1,0:T(8,128)S(1)} %collective-permute-done.5.refs_2_, f32[72,128]{1,0:T(8,128)S(1)} %collective-permute-done.6.refs_3_, bf16[2048,256]{1,0:T(8,128)(2,1)S(1)} %copy-done), custom_call_target="tpu_custom_call" | custom-call | tf_op jit(solution)/shard_map/pallas_call | solution.py:253
  23.6 3.9 %collective-permute-start.9 = (f32[4,256]{1,0:T(4,128)S(1)}, f32[4,256]{1,0:T(4,128)S(1)}, u32[]{:S(2)}, u32[]{:S(2)}) collective-permute-start(f32[4,256]{1,0:T(4,128)S(1)} %shard_map.59), channel_id=1, source_target_pairs={{0,2},{1,3},{2,0},{3,1},{4,6},{5,7},{6,4},{7,5},{8,10},{9,11},{10,... | collective-permute-start | bytes 12296 | tf_op jit(solution)/shard_map/ppermute | solution.py:265
  27.5 0.7 %collective-permute-start.8 = (f32[4,256]{1,0:T(4,128)S(1)}, f32[4,256]{1,0:T(4,128)S(1)}, u32[]{:S(2)}, u32[]{:S(2)}) collective-permute-start(f32[4,256]{1,0:T(4,128)S(1)} %shard_map.59), channel_id=1, source_target_pairs={{0,3},{1,2},{2,1},{3,0},{4,7},{5,6},{6,5},{7,4},{8,11},{9,10},{10,... | collective-permute-start | bytes 12296 | tf_op jit(solution)/shard_map/ppermute | solution.py:265
  28.2 0.3 collective-permute-start.7
  28.5 0.6 %collective-permute-done.9 = f32[4,256]{1,0:T(4,128)S(1)} collective-permute-done((f32[4,256]{1,0:T(4,128)S(1)}, f32[4,256]{1,0:T(4,128)S(1)}, u32[]{:S(2)}, u32[]{:S(2)}) %collective-permute-start.9) | collective-permute-done | bytes 4128 | tf_op jit(solution)/shard_map/ppermute | solution.py:265
  29.1 3.2 %collective-permute-done.8 = f32[4,256]{1,0:T(4,128)S(1)} collective-permute-done((f32[4,256]{1,0:T(4,128)S(1)}, f32[4,256]{1,0:T(4,128)S(1)}, u32[]{:S(2)}, u32[]{:S(2)}) %collective-permute-start.8) | collective-permute-done | bytes 4128 | tf_op jit(solution)/shard_map/ppermute | solution.py:265
  32.3 0.0 collective-permute-done.7
  32.3 0.6 %add_add_fusion = f32[4,256]{1,0:T(4,128)} fusion(f32[4,256]{1,0:T(4,128)S(1)} %collective-permute-done.9, f32[4,256]{1,0:T(4,128)S(1)} %collective-permute-done.8, f32[4,256]{1,0:T(4,128)S(1)} %shard_map.59, f32[4,256]{1,0:T(4,128)S(1)} %collective-permute-done.7), kind=kLoop, calls=%fused_computation | loop fusion | flops 3072 | bytes 20480 | tf_op jit(solution)/shard_map/add | solution.py:274
  (3 shorter events, 0.1 us)
Async XLA Ops:
  0.0 23.2 %copy-start = (bf16[2048,256]{1,0:T(8,128)(2,1)S(1)}, bf16[2048,256]{1,0:T(8,128)(2,1)}, u32[]{:S(2)}) copy-start(bf16[2048,256]{1,0:T(8,128)(2,1)} %refs_4_.1) | copy-start | bytes 3145732
  7.8 1.5 %collective-permute-start = (f32[72,128]{1,0:T(8,128)}, f32[72,128]{1,0:T(8,128)S(1)}, u32[]{:S(2)}, u32[]{:S(2)}) collective-permute-start(f32[72,128]{1,0:T(8,128)} %shard_map.55.source), channel_id=1, source_target_pairs={{0,4},{4,0},{8,12},{12,8},{16,20},{20,16},{24,28},{28,24},{32,36},... | collective-permute-start | bytes 110600 | tf_op jit(solution)/shard_map/ppermute | solution.py:265
  7.9 0.8 %copy-start.1 = (f32[72,128]{1,0:T(8,128)S(1)}, f32[72,128]{1,0:T(8,128)}, u32[]{:S(2)}) copy-start(f32[72,128]{1,0:T(8,128)} %shard_map.55.source) | copy-start | bytes 110596
  9.3 5.0 %collective-permute-start.3 = (f32[72,128]{1,0:T(8,128)S(1)}, f32[72,128]{1,0:T(8,128)S(1)}, u32[]{:S(2)}, u32[]{:S(2)}) collective-permute-start(f32[72,128]{1,0:T(8,128)S(1)} %shard_map.57.refs_0_), channel_id=1, source_target_pairs={{0,20},{4,16},{8,28},{12,24},{16,4},{20,0},{24,12},{28,8},{32,52},... | collective-permute-start | bytes 110600 | tf_op jit(solution)/shard_map/ppermute | solution.py:265
  12.4 4.6 %collective-permute-start.2 = (f32[72,128]{1,0:T(8,128)S(1)}, f32[72,128]{1,0:T(8,128)S(1)}, u32[]{:S(2)}, u32[]{:S(2)}) collective-permute-start(f32[72,128]{1,0:T(8,128)S(1)} %shard_map.57.refs_0_), channel_id=1, source_target_pairs={{0,28},{4,24},{8,20},{12,16},{16,12},{20,8},{24,4},{28,0},{32,60},... | collective-permute-start | bytes 110600 | tf_op jit(solution)/shard_map/ppermute | solution.py:265
  13.4 3.6 %collective-permute-start.1 = (f32[72,128]{1,0:T(8,128)S(1)}, f32[72,128]{1,0:T(8,128)S(1)}, u32[]{:S(2)}, u32[]{:S(2)}) collective-permute-start(f32[72,128]{1,0:T(8,128)S(1)} %shard_map.57.refs_0_), channel_id=1, source_target_pairs={{0,12},{4,8},{8,4},{12,0},{16,28},{20,24},{24,20},{28,16},{32,44},... | collective-permute-start | bytes 110600 | tf_op jit(solution)/shard_map/ppermute | solution.py:265
  17.1 3.9 %collective-permute-start.6 = (f32[72,128]{1,0:T(8,128)S(1)}, f32[72,128]{1,0:T(8,128)S(1)}, u32[]{:S(2)}, u32[]{:S(2)}) collective-permute-start(f32[72,128]{1,0:T(8,128)S(1)} %shard_map.58.refs_0_), channel_id=1, source_target_pairs={{0,36},{4,32},{8,44},{12,40},{16,52},{20,48},{24,60},{28,56},{32,4... | collective-permute-start | bytes 110600 | tf_op jit(solution)/shard_map/ppermute | solution.py:265
  18.2 4.6 %collective-permute-start.5 = (f32[72,128]{1,0:T(8,128)S(1)}, f32[72,128]{1,0:T(8,128)S(1)}, u32[]{:S(2)}, u32[]{:S(2)}) collective-permute-start(f32[72,128]{1,0:T(8,128)S(1)} %shard_map.58.refs_0_), channel_id=1, source_target_pairs={{0,100},{4,96},{8,108},{12,104},{16,116},{20,112},{24,124},{28,120... | collective-permute-start | bytes 110600 | tf_op jit(solution)/shard_map/ppermute | solution.py:265
  18.2 5.0 %collective-permute-start.4 = (f32[72,128]{1,0:T(8,128)S(1)}, f32[72,128]{1,0:T(8,128)S(1)}, u32[]{:S(2)}, u32[]{:S(2)}) collective-permute-start(f32[72,128]{1,0:T(8,128)S(1)} %shard_map.58.refs_0_), channel_id=1, source_target_pairs={{0,68},{4,64},{8,76},{12,72},{16,84},{20,80},{24,92},{28,88},{32,1... | collective-permute-start | bytes 110600 | tf_op jit(solution)/shard_map/ppermute | solution.py:265
  23.6 5.5 %collective-permute-start.9 = (f32[4,256]{1,0:T(4,128)S(1)}, f32[4,256]{1,0:T(4,128)S(1)}, u32[]{:S(2)}, u32[]{:S(2)}) collective-permute-start(f32[4,256]{1,0:T(4,128)S(1)} %shard_map.59), channel_id=1, source_target_pairs={{0,2},{1,3},{2,0},{3,1},{4,6},{5,7},{6,4},{7,5},{8,10},{9,11},{10,... | collective-permute-start | bytes 12296 | tf_op jit(solution)/shard_map/ppermute | solution.py:265
  27.5 4.8 %collective-permute-start.8 = (f32[4,256]{1,0:T(4,128)S(1)}, f32[4,256]{1,0:T(4,128)S(1)}, u32[]{:S(2)}, u32[]{:S(2)}) collective-permute-start(f32[4,256]{1,0:T(4,128)S(1)} %shard_map.59), channel_id=1, source_target_pairs={{0,3},{1,2},{2,1},{3,0},{4,7},{5,6},{6,5},{7,4},{8,11},{9,10},{10,... | collective-permute-start | bytes 12296 | tf_op jit(solution)/shard_map/ppermute | solution.py:265
  28.2 4.1 %collective-permute-start.7 = (f32[4,256]{1,0:T(4,128)S(1)}, f32[4,256]{1,0:T(4,128)S(1)}, u32[]{:S(2)}, u32[]{:S(2)}) collective-permute-start(f32[4,256]{1,0:T(4,128)S(1)} %shard_map.59), channel_id=1, source_target_pairs={{0,1},{1,0},{2,3},{3,2},{4,5},{5,4},{6,7},{7,6},{8,9},{9,8},{10,11... | collective-permute-start | bytes 12296 | tf_op jit(solution)/shard_map/ppermute | solution.py:265
where the time goes:
time: 33.3 us; the launch traced here: 32.9 us
  starting transfers between devices  13 us (39%)
  waiting for transfers between devices  10.3 us (31%)
  Pallas kernels  8.2 us (25%)
  local copies, waits for them, and re-layouts  0.76 us (2%)
  other arithmetic  0.6 us (2%)
    ppermute x10, starting transfers between devices, exchange(): lax.ppermute(value, axis, [(i, i ^ bit) for i in range(size)])  13 us
    ppermute x10, waiting for transfers between devices, exchange(): lax.ppermute(value, axis, [(i, i ^ bit) for i in range(size)])  10.3 us
    pallas_call x1, Pallas kernels, attention(): pl.pallas_call(attention_kernel, out_shape=jax.ShapeDtypeStruct((PACKED,...  7.77 us
    unnamed x4, local copies, waits for them, and re-layouts  0.76 us
  transfers between devices with their start and end apart: 10, of which 7 were waited for; matrix products, arithmetic and copies ran while one was open for 0% of the time, Pallas kernels for 0%

commit v1 on v0

--- a/solution.py
+++ b/solution.py
@@ -34,8 +34,9 @@
     query_copy = pltpu.make_async_copy(query_hbm, query, small_sem.at[0])
     lengths_copy.start()
     query_copy.start()
-    for c in range(2):
-        key_copy(0, c).start()
+    early = ((0, 0), (0, 1), (1, 0))
+    for r, c in early:
+        key_copy(r, c).start()
 
     offset = lax.axis_index("ctx") * ctx_dev
     lengths_copy.wait()
@@ -43,23 +44,22 @@
     for r in range(rows):
         order[count] = r
         count += (lengths[r] > offset).astype(jnp.int32)
-    first_ready = lengths[0] > offset
 
     def start_keys(i, c):
-        @pl.when(i < count)
+        r = order[i]
+        started = r < 2 if c == 0 else r < 1
+
+        @pl.when(jnp.logical_and(i < count, jnp.logical_not(started)))
         def _():
-            key_copy(order[i], c).start()
+            key_copy(r, c).start()
 
     def start_values(i, c):
         @pl.when(i < count)
         def _():
             value_copy(order[i], c).start()
 
-    @pl.when(jnp.logical_not(first_ready))
-    def _():
-        start_keys(0, 0)
-        start_keys(0, 1)
-
+    start_keys(0, 0)
+    start_keys(0, 1)
     for c in range(2):
         start_keys(1, c)
         start_values(0, c)
@@ -137,10 +137,11 @@
     value_copy(last, 1).wait()
     mix(last, 1)
 
-    @pl.when(jnp.logical_not(first_ready))
-    def _():
-        for c in range(2):
-            key_copy(0, c).wait()
+    for r, c in early:
+
+        @pl.when(lengths[r] <= offset)
+        def _(r=r, c=c):
+            key_copy(r, c).wait()
 
     top = jnp.maximum(tops[:, 0], tops[:, 1])
     scales = [jnp.exp2(tops[:, c] - top) for c in range(2)]
@@ -260,18 +261,32 @@
     )(*pieces, out_weight)
 
 
-def exchange(value, axis, bits):
-    size = lax.axis_size(axis)
-    return [value] + [lax.ppermute(value, axis, [(i, i ^ bit) for i in range(size)]) for bit in bits]
+def exchange(value, axis, perms):
+    return [value] + [lax.ppermute(value, axis, perm) for perm in perms]
+
+
+def along(axis, table):
+    perm = []
+    for x in range(4):
+        for y in range(4):
+            to_x, to_y = (table[x], y) if axis == "x" else (x, table[y])
+            perm += [((x * 4 + y) * 2 + core, (to_x * 4 + to_y) * 2 + 1 - core) for core in range(2)]
+    return perm
+
+
+CORE = [[(i, i ^ 1) for i in range(32)]]
+ALONG_Y = [along("y", table) for table in ((2, 0, 3, 1), (3, 2, 1, 0), (1, 3, 0, 2))]
+ALONG_X = [along("x", table) for table in ((2, 3, 0, 1), (3, 2, 1, 0), (1, 0, 3, 2))]
+ALONG_Z = [list(enumerate(table)) for table in ((2, 0, 3, 1), (3, 2, 1, 0), (1, 3, 0, 2))]
 
 
 def on_device(query, key_cache, cached_value_matrix, lengths, out_weight):
     rows = query.shape[0]
     packed = attention(query, key_cache, cached_value_matrix, lengths)
-    packed = merge_call([fetch(packed)] + exchange(packed, "ctx", (1,))[1:])
-    packed = merge_call(exchange(packed, "ctx", (3, 7, 5)))
-    partial_value = project_call(exchange(packed, "ctx", (17, 25, 9)), out_weight, rows)
-    return functools.reduce(jnp.add, exchange(partial_value, "head", (1, 3, 2)))
+    packed = merge_call([fetch(packed)] + exchange(packed, "ctx", CORE)[1:])
+    packed = merge_call(exchange(packed, "ctx", ALONG_Y))
+    partial_value = project_call(exchange(packed, "ctx", ALONG_X), out_weight, rows)
+    return functools.reduce(jnp.add, exchange(partial_value, "head", ALONG_Z))
 
 
 def solution(mesh):

time: 33.3 us -> 31.7 us (0.952)
  waiting for transfers between devices: 10.3 us -> 7.35 us
  starting transfers between devices: 13 us -> 14.5 us
    ppermute x10, waiting for transfers between devices: 10.3 us -> 7.35 us  [exchange(): return [value] + [lax.ppermute(value, axis, perm) for perm in perms]]
    ppermute x10, starting transfers between devices: 13 us -> 14.5 us  [exchange(): return [value] + [lax.ppermute(value, axis, perm) for perm in perms]]
  transfers between devices with their start and end apart: 10 -> 10, of which waited for: 7 -> 6; matrix products, arithmetic and copies ran while one was open for 0% -> 0% of each run, Pallas kernels for 0% -> 0%
where the time goes in v1:
time: 31.7 us; the launch traced here: 31.4 us
  starting transfers between devices  14.5 us (46%)
  Pallas kernels  8.13 us (26%)
  waiting for transfers between devices  7.35 us (23%)
  local copies, waits for them, and re-layouts  0.76 us (2%)
  other arithmetic  0.6 us (2%)
    ppermute x10, starting transfers between devices, exchange(): return [value] + [lax.ppermute(value, axis, perm) for perm in perms]  14.5 us
    pallas_call x1, Pallas kernels, attention(): pl.pallas_call(attention_kernel, out_shape=jax.ShapeDtypeStruct((PACKED,...  7.69 us
    ppermute x10, waiting for transfers between devices, exchange(): return [value] + [lax.ppermute(value, axis, perm) for perm in perms]  7.35 us
    unnamed x4, local copies, waits for them, and re-layouts  0.76 us
  transfers between devices with their start and end apart: 10, of which 6 were waited for; matrix products, arithmetic and copies ran while one was open for 0% of the time, Pallas kernels for 0%

profile of v1, /device:TPU:0, one launch (start us, length us, event | category | flops | bytes accessed | tf_op | source)
XLA Modules:
  0.0 31.4 jit_solution(2450115001651938171)
XLA Ops:
  0.0 0.0 copy-start
  0.0 7.7 %shard_map.55.source = f32[72,128]{1,0:T(8,128)} custom-call(s32[4]{0:T(128)} %lengths_hbm.1, bf16[4,2048]{1,0:T(4,128)(2,1)} %query_hbm.1, bf16[4,4096,256]{2,1,0:T(8,128)(2,1)} %key_hbm.1, bf16[4,4096,256]{2,1,0:T(8,128)(2,1)} %value_hbm.1), custom_call_target="tpu_custom_call" | custom-call | flops 268435456 | bytes 16777216 | tf_op jit(solution)/shard_map/pallas_call | solution.py:164
  7.7 0.1 collective-permute-start
  7.8 0.0 copy-start.1
  7.8 0.8 %copy-done.1 = f32[72,128]{1,0:T(8,128)S(1)} copy-done((f32[72,128]{1,0:T(8,128)S(1)}, f32[72,128]{1,0:T(8,128)}, u32[]{:S(2)}) %copy-start.1) | copy-done | bytes 36888
  8.6 0.6 %collective-permute-done.refs_1_ = f32[72,128]{1,0:T(8,128)S(1)} collective-permute-done((f32[72,128]{1,0:T(8,128)}, f32[72,128]{1,0:T(8,128)S(1)}, u32[]{:S(2)}, u32[]{:S(2)}) %collective-permute-start) | collective-permute-done | bytes 36896 | tf_op jit(solution)/shard_map/ppermute | solution.py:265
  9.2 1.5 %collective-permute-start.3 = (f32[72,128]{1,0:T(8,128)S(1)}, f32[72,128]{1,0:T(8,128)S(1)}, u32[]{:S(2)}, u32[]{:S(2)}) collective-permute-start(f32[72,128]{1,0:T(8,128)S(1)} %shard_map.57.refs_0_), channel_id=1, source_target_pairs={{0,12},{4,8},{8,28},{12,24},{16,4},{20,0},{24,20},{28,16},{32,44},... | collective-permute-start | bytes 110600 | tf_op jit(solution)/shard_map/ppermute | solution.py:265
  10.7 0.9 %collective-permute-start.2 = (f32[72,128]{1,0:T(8,128)S(1)}, f32[72,128]{1,0:T(8,128)S(1)}, u32[]{:S(2)}, u32[]{:S(2)}) collective-permute-start(f32[72,128]{1,0:T(8,128)S(1)} %shard_map.57.refs_0_), channel_id=1, source_target_pairs={{0,28},{4,24},{8,20},{12,16},{16,12},{20,8},{24,4},{28,0},{32,60},... | collective-permute-start | bytes 110600 | tf_op jit(solution)/shard_map/ppermute | solution.py:265
  11.7 1.2 %collective-permute-start.1 = (f32[72,128]{1,0:T(8,128)S(1)}, f32[72,128]{1,0:T(8,128)S(1)}, u32[]{:S(2)}, u32[]{:S(2)}) collective-permute-start(f32[72,128]{1,0:T(8,128)S(1)} %shard_map.57.refs_0_), channel_id=1, source_target_pairs={{0,20},{4,16},{8,4},{12,0},{16,28},{20,24},{24,12},{28,8},{32,52},... | collective-permute-start | bytes 110600 | tf_op jit(solution)/shard_map/ppermute | solution.py:265
  12.8 1.4 %collective-permute-done.3.refs_3_ = f32[72,128]{1,0:T(8,128)S(1)} collective-permute-done((f32[72,128]{1,0:T(8,128)S(1)}, f32[72,128]{1,0:T(8,128)S(1)}, u32[]{:S(2)}, u32[]{:S(2)}) %collective-permute-start.3) | collective-permute-done | bytes 36896 | tf_op jit(solution)/shard_map/ppermute | solution.py:265
  14.2 1.1 %collective-permute-done.2.refs_2_ = f32[72,128]{1,0:T(8,128)S(1)} collective-permute-done((f32[72,128]{1,0:T(8,128)S(1)}, f32[72,128]{1,0:T(8,128)S(1)}, u32[]{:S(2)}, u32[]{:S(2)}) %collective-permute-start.2) | collective-permute-done | bytes 36896 | tf_op jit(solution)/shard_map/ppermute | solution.py:265
  15.3 0.0 collective-permute-done.1.refs_1_
  15.3 0.1 collective-permute-start.6
  15.4 1.6 %collective-permute-start.5 = (f32[72,128]{1,0:T(8,128)S(1)}, f32[72,128]{1,0:T(8,128)S(1)}, u32[]{:S(2)}, u32[]{:S(2)}) collective-permute-start(f32[72,128]{1,0:T(8,128)S(1)} %shard_map.58.refs_0_), channel_id=1, source_target_pairs={{0,100},{4,96},{8,108},{12,104},{16,116},{20,112},{24,124},{28,120... | collective-permute-start | bytes 110600 | tf_op jit(solution)/shard_map/ppermute | solution.py:265
  17.0 2.1 %collective-permute-start.4 = (f32[72,128]{1,0:T(8,128)S(1)}, f32[72,128]{1,0:T(8,128)S(1)}, u32[]{:S(2)}, u32[]{:S(2)}) collective-permute-start(f32[72,128]{1,0:T(8,128)S(1)} %shard_map.58.refs_0_), channel_id=1, source_target_pairs={{0,68},{4,64},{8,76},{12,72},{16,84},{20,80},{24,92},{28,88},{32,1... | collective-permute-start | bytes 110600 | tf_op jit(solution)/shard_map/ppermute | solution.py:265
  19.2 0.0 collective-permute-done.6.refs_3_
  19.2 0.9 %collective-permute-done.5.refs_2_ = f32[72,128]{1,0:T(8,128)S(1)} collective-permute-done((f32[72,128]{1,0:T(8,128)S(1)}, f32[72,128]{1,0:T(8,128)S(1)}, u32[]{:S(2)}, u32[]{:S(2)}) %collective-permute-start.5) | collective-permute-done | bytes 36896 | tf_op jit(solution)/shard_map/ppermute | solution.py:265
  20.1 2.0 %collective-permute-done.4.refs_1_ = f32[72,128]{1,0:T(8,128)S(1)} collective-permute-done((f32[72,128]{1,0:T(8,128)S(1)}, f32[72,128]{1,0:T(8,128)S(1)}, u32[]{:S(2)}, u32[]{:S(2)}) %collective-permute-start.4) | collective-permute-done | bytes 36896 | tf_op jit(solution)/shard_map/ppermute | solution.py:265
  22.1 0.0 copy-done
  22.1 0.4 %shard_map.59 = f32[4,256]{1,0:T(4,128)S(1)} custom-call(f32[72,128]{1,0:T(8,128)S(1)} %shard_map.58.refs_0_, f32[72,128]{1,0:T(8,128)S(1)} %collective-permute-done.4.refs_1_, f32[72,128]{1,0:T(8,128)S(1)} %collective-permute-done.5.refs_2_, f32[72,128]{1,0:T(8,128)S(1)} %collective-permute-done.6.refs_3_, bf16[2048,256]{1,0:T(8,128)(2,1)S(1)} %copy-done), custom_call_target="tpu_custom_call" | custom-call | tf_op jit(solution)/shard_map/pallas_call | solution.py:254
  22.5 1.9 %collective-permute-start.9 = (f32[4,256]{1,0:T(4,128)S(1)}, f32[4,256]{1,0:T(4,128)S(1)}, u32[]{:S(2)}, u32[]{:S(2)}) collective-permute-start(f32[4,256]{1,0:T(4,128)S(1)} %shard_map.59), channel_id=1, source_target_pairs={{0,1},{1,3},{2,0},{3,2},{4,5},{5,7},{6,4},{7,6},{8,9},{9,11},{10,8... | collective-permute-start | bytes 12296 | tf_op jit(solution)/shard_map/ppermute | solution.py:265
  24.4 2.5 %collective-permute-start.8 = (f32[4,256]{1,0:T(4,128)S(1)}, f32[4,256]{1,0:T(4,128)S(1)}, u32[]{:S(2)}, u32[]{:S(2)}) collective-permute-start(f32[4,256]{1,0:T(4,128)S(1)} %shard_map.59), channel_id=1, source_target_pairs={{0,3},{1,2},{2,1},{3,0},{4,7},{5,6},{6,5},{7,4},{8,11},{9,10},{10,... | collective-permute-start | bytes 12296 | tf_op jit(solution)/shard_map/ppermute | solution.py:265
  27.0 2.5 %collective-permute-start.7 = (f32[4,256]{1,0:T(4,128)S(1)}, f32[4,256]{1,0:T(4,128)S(1)}, u32[]{:S(2)}, u32[]{:S(2)}) collective-permute-start(f32[4,256]{1,0:T(4,128)S(1)} %shard_map.59), channel_id=1, source_target_pairs={{0,2},{1,0},{2,3},{3,1},{4,6},{5,4},{6,7},{7,5},{8,10},{9,8},{10,1... | collective-permute-start | bytes 12296 | tf_op jit(solution)/shard_map/ppermute | solution.py:265
  29.5 0.0 collective-permute-done.9
  29.5 0.0 collective-permute-done.8
  29.5 1.3 %collective-permute-done.7 = f32[4,256]{1,0:T(4,128)S(1)} collective-permute-done((f32[4,256]{1,0:T(4,128)S(1)}, f32[4,256]{1,0:T(4,128)S(1)}, u32[]{:S(2)}, u32[]{:S(2)}) %collective-permute-start.7) | collective-permute-done | bytes 4128 | tf_op jit(solution)/shard_map/ppermute | solution.py:265
  30.8 0.6 %add_add_fusion = f32[4,256]{1,0:T(4,128)} fusion(f32[4,256]{1,0:T(4,128)S(1)} %collective-permute-done.9, f32[4,256]{1,0:T(4,128)S(1)} %collective-permute-done.8, f32[4,256]{1,0:T(4,128)S(1)} %shard_map.59, f32[4,256]{1,0:T(4,128)S(1)} %collective-permute-done.7), kind=kLoop, calls=%fused_computation | loop fusion | flops 3072 | bytes 20480 | tf_op jit(solution)/shard_map/add | solution.py:289
  (3 shorter events, 0.1 us)
Async XLA Ops:
  0.0 22.1 %copy-start = (bf16[2048,256]{1,0:T(8,128)(2,1)S(1)}, bf16[2048,256]{1,0:T(8,128)(2,1)}, u32[]{:S(2)}) copy-start(bf16[2048,256]{1,0:T(8,128)(2,1)} %refs_4_.1) | copy-start | bytes 3145732
  7.7 1.5 %collective-permute-start = (f32[72,128]{1,0:T(8,128)}, f32[72,128]{1,0:T(8,128)S(1)}, u32[]{:S(2)}, u32[]{:S(2)}) collective-permute-start(f32[72,128]{1,0:T(8,128)} %shard_map.55.source), channel_id=1, source_target_pairs={{0,4},{4,0},{8,12},{12,8},{16,20},{20,16},{24,28},{28,24},{32,36},... | collective-permute-start | bytes 110600 | tf_op jit(solution)/shard_map/ppermute | solution.py:265
  7.8 0.8 %copy-start.1 = (f32[72,128]{1,0:T(8,128)S(1)}, f32[72,128]{1,0:T(8,128)}, u32[]{:S(2)}) copy-start(f32[72,128]{1,0:T(8,128)} %shard_map.55.source) | copy-start | bytes 110596
  9.2 5.0 %collective-permute-start.3 = (f32[72,128]{1,0:T(8,128)S(1)}, f32[72,128]{1,0:T(8,128)S(1)}, u32[]{:S(2)}, u32[]{:S(2)}) collective-permute-start(f32[72,128]{1,0:T(8,128)S(1)} %shard_map.57.refs_0_), channel_id=1, source_target_pairs={{0,12},{4,8},{8,28},{12,24},{16,4},{20,0},{24,20},{28,16},{32,44},... | collective-permute-start | bytes 110600 | tf_op jit(solution)/shard_map/ppermute | solution.py:265
  10.7 4.6 %collective-permute-start.2 = (f32[72,128]{1,0:T(8,128)S(1)}, f32[72,128]{1,0:T(8,128)S(1)}, u32[]{:S(2)}, u32[]{:S(2)}) collective-permute-start(f32[72,128]{1,0:T(8,128)S(1)} %shard_map.57.refs_0_), channel_id=1, source_target_pairs={{0,28},{4,24},{8,20},{12,16},{16,12},{20,8},{24,4},{28,0},{32,60},... | collective-permute-start | bytes 110600 | tf_op jit(solution)/shard_map/ppermute | solution.py:265
  11.7 3.7 %collective-permute-start.1 = (f32[72,128]{1,0:T(8,128)S(1)}, f32[72,128]{1,0:T(8,128)S(1)}, u32[]{:S(2)}, u32[]{:S(2)}) collective-permute-start(f32[72,128]{1,0:T(8,128)S(1)} %shard_map.57.refs_0_), channel_id=1, source_target_pairs={{0,20},{4,16},{8,4},{12,0},{16,28},{20,24},{24,12},{28,8},{32,52},... | collective-permute-start | bytes 110600 | tf_op jit(solution)/shard_map/ppermute | solution.py:265
  15.3 3.9 %collective-permute-start.6 = (f32[72,128]{1,0:T(8,128)S(1)}, f32[72,128]{1,0:T(8,128)S(1)}, u32[]{:S(2)}, u32[]{:S(2)}) collective-permute-start(f32[72,128]{1,0:T(8,128)S(1)} %shard_map.58.refs_0_), channel_id=1, source_target_pairs={{0,36},{4,32},{8,44},{12,40},{16,52},{20,48},{24,60},{28,56},{32,4... | collective-permute-start | bytes 110600 | tf_op jit(solution)/shard_map/ppermute | solution.py:265
  15.4 4.7 %collective-permute-start.5 = (f32[72,128]{1,0:T(8,128)S(1)}, f32[72,128]{1,0:T(8,128)S(1)}, u32[]{:S(2)}, u32[]{:S(2)}) collective-permute-start(f32[72,128]{1,0:T(8,128)S(1)} %shard_map.58.refs_0_), channel_id=1, source_target_pairs={{0,100},{4,96},{8,108},{12,104},{16,116},{20,112},{24,124},{28,120... | collective-permute-start | bytes 110600 | tf_op jit(solution)/shard_map/ppermute | solution.py:265
  17.0 5.1 %collective-permute-start.4 = (f32[72,128]{1,0:T(8,128)S(1)}, f32[72,128]{1,0:T(8,128)S(1)}, u32[]{:S(2)}, u32[]{:S(2)}) collective-permute-start(f32[72,128]{1,0:T(8,128)S(1)} %shard_map.58.refs_0_), channel_id=1, source_target_pairs={{0,68},{4,64},{8,76},{12,72},{16,84},{20,80},{24,92},{28,88},{32,1... | collective-permute-start | bytes 110600 | tf_op jit(solution)/shard_map/ppermute | solution.py:265
  22.5 7.0 %collective-permute-start.9 = (f32[4,256]{1,0:T(4,128)S(1)}, f32[4,256]{1,0:T(4,128)S(1)}, u32[]{:S(2)}, u32[]{:S(2)}) collective-permute-start(f32[4,256]{1,0:T(4,128)S(1)} %shard_map.59), channel_id=1, source_target_pairs={{0,1},{1,3},{2,0},{3,2},{4,5},{5,7},{6,4},{7,6},{8,9},{9,11},{10,8... | collective-permute-start | bytes 12296 | tf_op jit(solution)/shard_map/ppermute | solution.py:265
  24.4 5.1 %collective-permute-start.8 = (f32[4,256]{1,0:T(4,128)S(1)}, f32[4,256]{1,0:T(4,128)S(1)}, u32[]{:S(2)}, u32[]{:S(2)}) collective-permute-start(f32[4,256]{1,0:T(4,128)S(1)} %shard_map.59), channel_id=1, source_target_pairs={{0,3},{1,2},{2,1},{3,0},{4,7},{5,6},{6,5},{7,4},{8,11},{9,10},{10,... | collective-permute-start | bytes 12296 | tf_op jit(solution)/shard_map/ppermute | solution.py:265
  27.0 3.9 %collective-permute-start.7 = (f32[4,256]{1,0:T(4,128)S(1)}, f32[4,256]{1,0:T(4,128)S(1)}, u32[]{:S(2)}, u32[]{:S(2)}) collective-permute-start(f32[4,256]{1,0:T(4,128)S(1)} %shard_map.59), channel_id=1, source_target_pairs={{0,2},{1,0},{2,3},{3,1},{4,6},{5,4},{6,7},{7,5},{8,10},{9,8},{10,1... | collective-permute-start | bytes 12296 | tf_op jit(solution)/shard_map/ppermute | solution.py:265
